TPU v7x, 128 devices: a whole 4x4x4 slice. The times are simulated.
128 devices in a mesh: dp: 8 (over x_lo, z), tile: 16 (over x_hi, y, core).
Axes of the slice: x: 4 (x_hi: 2, x_lo: 2; x = x_hi * 2 + x_lo), y: 4, z: 4, core: 2. Of those that a mesh axis runs over, the one named last changes fastest.
Arguments:
- gradient: bfloat16 [9216, 7168], P('dp', 'tile'), may hold values from -0.1875 to 0.1875
- stats_old: float32 [7168, 7168], P('dp', 'tile'), as said below
- owner_map: int32 [8, 16], P('dp'), may hold values from 0 to 15, as said below
Outputs:
- refreshed: float32 [7168, 7168], P('dp', 'tile')
- owned_rows: float32 [256, 56, 7168], P(('dp', 'tile'))
Inputs may be any that keep to these rules, and one draw needn't show every extreme that they name: `owner_map`: in each row group no tile index owns more than 2 row units, and some tile index owns exactly 2. `stats_old`: Symmetric.
All inputs are finite; a program needn't handle non-finite values.
Results may differ from a plain program's by a relative error of at most 0.0003.
Values may be sent and summed in bfloat16 or wider, within the bound.
A program may use at most 192 MiB of HBM per device.

v0:
```python
import jax
import jax.numpy as jnp
from jax import lax
from jax.sharding import PartitionSpec as P

CAP = 2


EMA_DECAY = 0.9


def slot_select(owners, count, slots):
    position = jnp.arange(count, dtype=jnp.int32)
    matches = owners[:, None] == owners[None, :]
    earlier = position[None, :] < position[:, None]
    ranking = jnp.sum((matches & earlier).astype(jnp.int32), axis=1)
    chosen = (owners[None, None, :] == position[None, :, None]) & (
        ranking[None, None, :] == jnp.arange(slots, dtype=jnp.int32)[:, None, None]
    )
    return chosen.astype(jnp.float32)


def gram_block(left_part, right_part):
    return lax.dot_general(
        left_part, right_part, (((0,), (0,)), ((), ())), preferred_element_type=jnp.float32
    )


def local(gradient, stats_old, owner_map):
    block_width = gradient.shape[1]
    tile_count = lax.axis_size("tile")
    full_width = block_width * tile_count
    share_rows = full_width // lax.axis_size("dp")
    gathered = lax.all_gather(gradient, "tile", axis=1, tiled=True)
    summed = lax.psum_scatter(gram_block(gathered, gradient), "dp", scatter_dimension=0, tiled=True)
    refreshed = EMA_DECAY * stats_old + (1.0 - EMA_DECAY) * summed
    unit_height = share_rows // tile_count
    unit_rows = refreshed.reshape(tile_count, unit_height, block_width)
    selection = slot_select(owner_map[0], tile_count, CAP)
    outgoing = jnp.einsum("seu,urc->srec", selection, unit_rows, precision=lax.Precision.HIGHEST)
    incoming = lax.all_to_all(outgoing, "tile", split_axis=2, concat_axis=2, tiled=True)
    return (refreshed, incoming.reshape(CAP, unit_height, full_width))


def solution(mesh):
    return jax.shard_map(
        local,
        mesh=mesh,
        in_specs=(P("dp", "tile"), P("dp", "tile"), P("dp", None)),
        out_specs=(P("dp", "tile"), P(("dp", "tile"), None, None)),
        check_vma=False,
    )
```

profile of v0, /device:TPU:24, one launch (start us, length us, event | category | flops | bytes accessed | tf_op | source)
XLA Modules:
  0.0 343.1 jit_solution(4768395497760905028)
XLA Ops:
  7.2 0.0 all-gather.2.cloned.1.call-start
  7.2 0.7 all-gather.2.cloned.1.call-update
  7.9 0.0 reduce-scatter.2.cloned.1.call-start
  7.9 110.7 %all-gather.2.cloned.1.call-done = bf16[1152,7168]{0,1:T(8,128)(2,1)} async-done(((bf16[1152,448]{0,1:T(8,128)(2,1)}), bf16[1152,7168]{0,1:T(8,128)(2,1)}) %all-gather.2.cloned.1.call-update) | async-done | bytes 16515088 | tf_op jit(solution)/shard_map/all_gather | solution.py:34
  118.6 15.0 %fusion.6 = f32[7168,448]{0,1:T(8,128)} fusion(bf16[1152,7168]{0,1:T(8,128)(2,1)} %all-gather.2.cloned.1.call-done, bf16[1152,448]{0,1:T(8,128)(2,1)} %param.3), kind=kOutput, calls=%fused_computation.12 | convolution fusion | flops 7398752256 | bytes 30392320 | tf_op jit(solution)/shard_map/dot_general | solution.py:24
  133.6 0.0 copy-start.2
  133.6 0.0 copy-start.1
  133.6 0.0 reduce-scatter.2.cloned.1.call-update
  133.6 0.6 copy-done.2
  134.3 0.2 convert_reduce_fusion
  134.5 133.9 %reduce-scatter.2.cloned.1.call-done = f32[896,448]{0,1:T(8,128)} async-done(((f32[7168,448]{0,1:T(8,128)}), f32[896,448]{0,1:T(8,128)}) %reduce-scatter.2.cloned.1.call-update) | async-done | bytes 1605648 | tf_op jit(solution)/shard_map/reduce_scatter | solution.py:35
  268.4 0.0 copy-done.1
  268.4 1.7 multiply_add_fusion
  270.1 0.0 copy-start
  270.1 0.8 copy.13
  270.9 2.7 convolution_bitcast_fusion
  273.6 0.0 copy-done
  273.7 2.8 copy.15
  276.5 50.6 %all_to_all.5 = f32[2,56,16,448]{3,0,1,2:T(2,128)S(1)} all-to-all(f32[2,56,16,448]{3,0,1,2:T(2,128)S(1)} %copy.15), channel_id=1, replica_groups=mesh['dp'=8,'tile'=16] {'tile'}, dimensions={2} | all-to-all | bytes 6422528 | tf_op jit(solution)/shard_map/all_to_all | solution.py:41
  327.1 3.9 %copy.16 = f32[2,56,16,448]{3,2,1,0:T(8,128)} copy(f32[2,56,16,448]{3,0,1,2:T(2,128)S(1)} %all_to_all.5) | data formatting | bytes 6422528 | tf_op jit(solution)/shard_map/all_to_all | solution.py:41
  331.0 5.2 %reshape.60 = f32[2,56,7168]{2,1,0:T(8,128)} reshape(f32[2,56,16,448]{3,2,1,0:T(8,128)} %copy.16) | data formatting | bytes 6422528 | tf_op jit(solution)/shard_map/reshape | solution.py:42
  (2 shorter events, 0.0 us)
Async XLA Ops:
  7.2 111.5 %all-gather.2.cloned.1.call-start = ((), (), s32[]{:S(2)}) async-start(), calls=%async_computation.2 | async-start | bytes 17547264 | tf_op jit(solution)/shard_map/all_gather | solution.py:34
  7.9 260.5 %reduce-scatter.2.cloned.1.call-start = ((), (), s32[]{:S(2)}) async-start(), calls=%async_computation.3 | async-start | bytes 14450688 | tf_op jit(solution)/shard_map/reduce_scatter | solution.py:35
  133.6 0.7 copy-start.2
  133.6 134.8 %copy-start.1 = (f32[896,448]{0,1:T(8,128)S(1)}, f32[896,448]{0,1:T(8,128)}, u32[]{:S(2)}) copy-start(f32[896,448]{0,1:T(8,128)} %param.4) | copy-start | bytes 4816900
  270.1 3.6 %copy-start = (f32[896,448]{0,1:T(8,128)}, f32[896,448]{0,1:T(8,128)S(1)}, u32[]{:S(2)}) copy-start(f32[896,448]{0,1:T(8,128)S(1)} %multiply_add_fusion) | copy-start | bytes 4816900
Sparse Core Ops, SparseCore 0:
  10.5 108.0 all-gather.1
  133.7 134.5 reduce-scatter.1
where the time goes:
time: 346 us; the launch traced here: 343 us
  waiting for transfers between devices  245 us (71%)
  blocking collectives  50.6 us (15%)
  matrix products  17.7 us (5%)
  between operations  14.1 us (4%)
  local copies, waits for them, and re-layouts  13.4 us (4%)
    reduce_scatter x1, waiting for transfers between devices, local(): lax.psum_scatter(gram_block(gathered, gradient), 'dp', scatter_dimension=...  134 us
    all_gather x1, waiting for transfers between devices, local(): gathered = lax.all_gather(gradient, 'tile', axis=1, tiled=True)  111 us
    all_to_all x1, blocking collectives, local(): lax.all_to_all(outgoing, 'tile', split_axis=2, concat_axis=2, tiled=True)  50.6 us
    dot_general x1, matrix products, gram_block(): lax.dot_general(left_part, right_part, (((0,), (0,)), ((), ())), preferre...  15 us
  transfers between devices with their start and end apart: 2, of which 2 were waited for; matrix products, arithmetic and copies ran while one was open for 0% of the time, Pallas kernels for 0%

commit v1 on v0

v1 whole, which is shorter than its diff:
```python
import functools

import jax
import jax.numpy as jnp
from jax import lax
from jax.experimental import pallas as pl
from jax.experimental.pallas import tpu as pltpu
from jax.sharding import PartitionSpec as P

MESH = pl.DeviceIdType.MESH
EMA_DECAY = 0.9
Q = 7
LEVELS = 32767.0


def kernel(grad, stats, owner, refreshed, owned, cols, rows, prod, zin, coded, out16, in16,
           c_s, c_r, b_s, b_r, y_s, y_r, f_s, f_r, k_s, k_r, z_s, z_r, o_s, o_r):
    depth, width = grad.shape
    high = width // Q
    unit = owned.shape[1]
    dp, tile = lax.axis_index("dp"), lax.axis_index("tile")
    a, z = dp // 4, dp % 4
    b, y, core = tile // 8, (tile // 2) % 4, tile % 2
    middle = a != b

    def at(a_, z_, b_, y_, core_):
        return {"dp": a_ * 4 + z_, "tile": b_ * 8 + y_ * 2 + core_}

    partner = at(1 - a, z, b, y, core)
    bridge = at(1 - a, z, 1 - b, y, core)
    sibling = at(a, z, b, y, 1 - core)
    yu, yd, yo = (y + 1) % 4, (y + 3) % 4, (y + 2) % 4
    zu, zd, zo = (z + 1) % 4, (z + 3) % 4, (z + 2) % 4
    up_y, down_y = at(a, z, b, yu, core), at(a, z, b, yd, core)
    up_z, down_z = at(a, zu, b, y, core), at(a, zd, b, y, core)

    def copy(src, dst, send, recv, device):
        return pltpu.make_async_remote_copy(
            src_ref=src, dst_ref=dst, send_sem=send, recv_sem=recv, device_id=device, device_id_type=MESH
        )

    def c_copy(q, p):
        part = cols.at[p, pl.ds(q * high, high)]
        return copy(part, part, c_s.at[q], c_r.at[q], partner)

    def b_copy(q, p, which):
        return copy(cols.at[p, pl.ds(q * high, high)], rows.at[q, core, y, p], b_s.at[q, which], b_r.at[q, which], bridge)

    def y_copy(q, which):
        part = rows.at[q, core, y]
        return copy(part, part, y_s.at[q, which], y_r.at[q, which], up_y if which else down_y)

    def y_arrived(q, which):
        part = rows.at[q, core, yd if which else yu]
        return copy(part, part, y_s.at[q, which], y_r.at[q, which], up_y if which else down_y)

    def f_copy(q, which):
        part = rows.at[q, core, yd if which else yu, which]
        return copy(part, part, f_s.at[q, which], f_r.at[q, which], up_y if which else down_y)

    def f_arrived(q, which):
        part = rows.at[q, core, yo, which]
        return copy(part, part, f_s.at[q, which], f_r.at[q, which], up_y if which else down_y)

    def k_copy(q, half):
        part = rows.at[q, half]
        return copy(part, part, k_s.at[q], k_r.at[q], sibling)

    def z_copy(q, slot):
        half, dest, device = {
            0: (0, zu, up_z), 1: (1, zu, up_z), 2: (0, zd, down_z), 3: (1, zd, down_z), 4: (1, zo, up_z), 5: (0, zo, down_z),
        }[slot]
        return copy(prod.at[q, half, dest], zin.at[q, slot], z_s.at[q, slot], z_r.at[q, slot], device)

    def o_copy(e):
        return copy(out16.at[e], in16.at[tile], o_s.at[e], o_r.at[tile], {"tile": e})

    def o_arrived(e):
        return copy(out16.at[e], in16.at[e], o_s.at[e], o_r.at[e], {"tile": e})

    barrier = pltpu.get_barrier_semaphore()

    def greet(e, _):
        @pl.when(e != tile)
        def _():
            pl.semaphore_signal(barrier, inc=1, device_id={"tile": e}, device_id_type=MESH)
        return 0

    for device in (partner, bridge, up_z, down_z):
        pl.semaphore_signal(barrier, inc=1, device_id=device, device_id_type=MESH)
    lax.fori_loop(0, 16, greet, 0)

    block = 0
    begun = False
    while block < width:
        wide = min(128, width - block)
        cols[a, block:block + wide, :] = grad[:, block:block + wide].T
        if not begun:
            pl.semaphore_wait(barrier, 19)
            begun = True
        for q in range(block // high, (block + wide) // high):
            c_copy(q, a).start()

            @pl.when(middle)
            def _(q=q):
                b_copy(q, a, 0).start()
        block += wide

    def c_step(q):
        c_copy(q, 1 - a).wait_recv()

        @pl.when(middle)
        def _():
            b_copy(q, 1 - a, 1).start()

        @pl.when(jnp.logical_not(middle))
        def _():
            for p in range(2):
                rows[q, core, y, p] = cols[p, pl.ds(pl.multiple_of(q * high, high), high), :]

    def e1(q):
        @pl.when(middle)
        def _():
            for which in range(2):
                b_copy(q, a, which).wait_recv()
        for which in range(2):
            y_copy(q, which).start()

    def e2(q):
        for which in range(2):
            y_arrived(q, which).wait_recv()
            f_copy(q, which).start()

    def e3(q):
        for which in range(2):
            f_arrived(q, which).wait_recv()
        k_copy(q, core).start()

    def e4(q):
        k_copy(q, 1 - core).wait_recv()
        for half in range(2):
            total = None
            for p in range(2):
                left = rows[q, half, :, p].reshape(4 * high, depth)
                part = lax.dot_general(left, cols[p], (((1,), (1,)), ((), ())), preferred_element_type=jnp.float32)
                total = part if total is None else total + part
            prod[q, half] = total.reshape(4, high, width)
        for slot in (4, 5, 0, 3):
            z_copy(q, slot).start()

    def e5(q):
        z_copy(q, 4).wait_recv()
        prod[q, 1, zu] += zin[q, 4]
        z_copy(q, 1).start()
        z_copy(q, 5).wait_recv()
        prod[q, 0, zd] += zin[q, 5]
        z_copy(q, 2).start()

    def e6(q):
        for slot in range(4):
            z_copy(q, slot).wait_recv()
        for half in range(2):
            place = pl.ds(pl.multiple_of(half * width + q * high, 8), high)
            summed = prod[q, half, z] + zin[q, half] + zin[q, 2 + half]
            refreshed[place, :] = EMA_DECAY * stats[place, :] + (1.0 - EMA_DECAY) * summed

    def step(i, _):
        for k in range(2):
            pl.when(2 * i + k < Q)(functools.partial(c_step, 2 * i + k))
        pl.when(i < Q)(functools.partial(e1, i))
        pl.when((i >= 1) & (i < Q + 1))(functools.partial(e2, i - 1))
        pl.when((i >= 2) & (i < Q + 2))(functools.partial(e3, i - 2))
        pl.when((i >= 3) & (i < Q + 3))(functools.partial(e5, i - 3))
        pl.when((i >= 4) & (i < Q + 4))(functools.partial(e6, i - 4))
        pl.when((i >= 2) & (i < Q + 2))(functools.partial(e4, i - 2))
        return 0

    lax.fori_loop(0, 2, step, 0)
    for q in range(4, Q):
        c_step(q)

    def late(i, _):
        pl.when(i < Q)(functools.partial(e1, i))
        pl.when(i < Q + 1)(functools.partial(e2, i - 1))
        pl.when(i < Q + 2)(functools.partial(e3, i - 2))
        pl.when((i >= 3) & (i < Q + 3))(functools.partial(e5, i - 3))
        pl.when(i >= 4)(functools.partial(e6, i - 4))
        pl.when(i < Q + 2)(functools.partial(e4, i - 2))
        return 0

    lax.fori_loop(2, Q + 4, late, 0)

    def encode(u, _):
        values = refreshed[pl.ds(pl.multiple_of(u * unit, 8), unit), :]
        for first in range(0, width, 128):
            last = min(first + 128, width)
            part = values[:, first:last]
            most = jnp.maximum(jnp.max(jnp.abs(part), axis=1, keepdims=True), 2.0 ** -100)
            power = jnp.ceil(8.0 * jnp.log2(most))
            part = jnp.clip(part * (jnp.exp2(power * -0.125) * LEVELS), -LEVELS, LEVELS)
            coded[u, :, first:last] = jnp.round(part)
            place = width + 16 * (first // 128)
            coded[u, :, place:place + 16] = jnp.broadcast_to(power, (unit, 16))
        return 0

    lax.fori_loop(0, 16, encode, 0)

    def send(j, _):
        e = (tile + 1 + j) % 16
        count, first, second = jnp.int32(0), jnp.int32(0), jnp.int32(0)
        for u in range(16):
            mine = (owner[0, u] == e).astype(jnp.int32)
            first = first + jnp.where(count == 0, mine * u, 0)
            second = second + jnp.where(count == 1, mine * u, 0)
            count = count + mine
        pieces = [coded[u] * (count > s).astype(jnp.float32) for s, u in enumerate((first, second))]
        out16[e] = jnp.concatenate(pieces, axis=0).astype(jnp.int32).astype(jnp.int16)

        @pl.when(j < 15)
        def _():
            o_copy(e).start()
        return 0

    lax.fori_loop(0, 16, send, 0)
    in16[tile] = out16[tile]

    def await_owned(j, _):
        o_arrived((tile + 15 - j) % 16).wait_recv()
        return 0

    lax.fori_loop(0, 15, await_owned, 0)
    for pair in range(8):
        parts = []
        for k in range(2):
            got = in16[2 * pair + k].astype(jnp.int32).astype(jnp.float32)
            pieces = []
            for first in range(0, width, 128):
                place = width + 16 * (first // 128)
                scale = jnp.exp2(got[:, place:place + 1] * 0.125) * (1.0 / LEVELS)
                pieces.append(got[:, first:min(first + 128, width)] * scale)
            parts.append(jnp.concatenate(pieces, axis=1))
        both = jnp.concatenate(parts, axis=1)
        for s in range(2):
            owned[s, :, pair * 2 * width:(pair + 1) * 2 * width] = both[s * unit:(s + 1) * unit]

    def drain(q, _):
        c_copy(q, a).wait_send()

        @pl.when(middle)
        def _():
            b_copy(q, a, 0).wait_send()
            b_copy(q, 1 - a, 1).wait_send()
        for which in range(2):
            y_copy(q, which).wait_send()
            f_copy(q, which).wait_send()
        k_copy(q, core).wait_send()
        for slot in range(6):
            z_copy(q, slot).wait_send()
        return 0

    lax.fori_loop(0, Q, drain, 0)

    def drain_owned(j, _):
        o_copy((tile + 1 + j) % 16).wait_send()
        return 0

    lax.fori_loop(0, 15, drain_owned, 0)


def local(gradient, stats_old, owner_map):
    depth, width = gradient.shape
    high = width // Q
    rows = stats_old.shape[0]
    unit = rows // 16
    dma = pltpu.SemaphoreType.DMA
    vmem = pl.BlockSpec(memory_space=pltpu.VMEM)
    return pl.pallas_call(
        kernel,
        out_shape=(
            jax.ShapeDtypeStruct((rows, width), jnp.float32),
            jax.ShapeDtypeStruct((2, unit, 16 * width), jnp.float32),
        ),
        in_specs=[vmem, vmem, pl.BlockSpec(memory_space=pltpu.SMEM)],
        out_specs=(vmem, vmem),
        scratch_shapes=[
            pltpu.VMEM((2, width, depth), jnp.bfloat16),
            pltpu.VMEM((Q, 2, 4, 2, high, depth), jnp.bfloat16),
            pltpu.VMEM((Q, 2, 4, high, width), jnp.float32),
            pltpu.VMEM((Q, 6, high, width), jnp.float32),
            pltpu.VMEM((16, unit, 512), jnp.float32),
            pltpu.VMEM((16, 2 * unit, 512), jnp.int16),
            pltpu.VMEM((16, 2 * unit, 512), jnp.int16),
            dma((Q,)), dma((Q,)),
            dma((Q, 2)), dma((Q, 2)),
            dma((Q, 2)), dma((Q, 2)),
            dma((Q, 2)), dma((Q, 2)),
            dma((Q,)), dma((Q,)),
            dma((Q, 6)), dma((Q, 6)),
            dma((16,)), dma((16,)),
        ],
        compiler_params=pltpu.CompilerParams(
            collective_id=0, has_side_effects=True, vmem_limit_bytes=60 << 20
        ),
    )(gradient, stats_old, owner_map)


def solution(mesh):
    return jax.shard_map(
        local,
        mesh=mesh,
        in_specs=(P("dp", "tile"), P("dp", "tile"), P("dp", None)),
        out_specs=(P("dp", "tile"), P(("dp", "tile"), None, None)),
        check_vma=False,
    )
```

time: 346 us -> 170 us (0.49)
  waiting for transfers between devices: 245 us -> 0 us
  Pallas kernels: 0 us -> 158 us
  blocking collectives: 50.6 us -> 0 us
  matrix products: 17.7 us -> 0 us
  between operations: 14.1 us -> 0.66 us
  local copies, waits for them, and re-layouts: 13.4 us -> 8.7 us
    pallas_call x0 -> x1, Pallas kernels: none -> 158 us  [local(): pl.pallas_call(kernel, out_shape=(jax.ShapeDtypeStruct((rows, width), jnp...]
    reduce_scatter x1 -> x0, waiting for transfers between devices: 134 us -> none  [local(): lax.psum_scatter(gram_block(gathered, gradient), 'dp', scatter_dimension=...]
    all_gather x1 -> x0, waiting for transfers between devices: 111 us -> none  [local(): gathered = lax.all_gather(gradient, 'tile', axis=1, tiled=True)]
    all_to_all x1 -> x0, blocking collectives: 50.6 us -> none  [local(): lax.all_to_all(outgoing, 'tile', split_axis=2, concat_axis=2, tiled=True)]
    dot_general x2 -> x0, matrix products: 17.7 us -> none  [the longest x1 15 us: gram_block(): lax.dot_general(left_part, right_part, (((0,), (0,)), ((), ())), preferre...]
    unnamed x6 -> x7, local copies, waits for them, and re-layouts: 0.64 us -> 5.9 us
    reshape x1 -> x0, local copies, waits for them, and re-layouts: 5.22 us -> none  [local(): return (refreshed, incoming.reshape(CAP, unit_height, full_width))]
    all_to_all x1 -> x0, local copies, waits for them, and re-layouts: 3.91 us -> none  [local(): lax.all_to_all(outgoing, 'tile', split_axis=2, concat_axis=2, tiled=True)]
  transfers between devices with their start and end apart: 2 -> 0, of which waited for: 2 -> 0; matrix products, arithmetic and copies ran while one was open for 0% -> 0% of each run, Pallas kernels for 0% -> 0%
where the time goes in v1:
time: 170 us; the launch traced here: 168 us
  Pallas kernels  158 us (93%)
  local copies, waits for them, and re-layouts  8.7 us (5%)
    pallas_call x1, Pallas kernels, local(): pl.pallas_call(kernel, out_shape=(jax.ShapeDtypeStruct((rows, width), jnp...  158 us
    unnamed x7, local copies, waits for them, and re-layouts  5.9 us

profile of v1, /device:TPU:24, one launch (start us, length us, event | category | flops | bytes accessed | tf_op | source)
XLA Modules:
  0.0 167.6 jit_solution(12238384608801991735)
XLA Ops:
  0.6 0.0 copy-start.1
  0.6 2.5 %copy.5.grad = bf16[1152,448]{1,0:T(8,128)(2,1)} copy(bf16[1152,448]{0,1:T(8,128)(2,1)} %param.3) | data formatting | bytes 2064384 | tf_op args[0]
  3.1 0.0 copy-done.1
  3.1 1.7 %copy.6.stats = f32[896,448]{1,0:T(8,128)} copy(f32[896,448]{0,1:T(8,128)S(1)} %copy-done.1) | data formatting | bytes 3211264 | tf_op args[1]
  4.8 158.2 %shard_map.50 = (f32[896,448]{1,0:T(8,128)}, f32[2,56,7168]{2,1,0:T(8,128)}) custom-call(bf16[1152,448]{1,0:T(8,128)(2,1)} %copy.5.grad, f32[896,448]{1,0:T(8,128)} %copy.6.stats, s32[1,16]{1,0:T(1,128)} %owner.1), custom_call_target="tpu_custom_call" | custom-call | tf_op jit(solution)/shard_map/pallas_call | solution.py:277
  163.1 0.0 copy-start
  163.1 2.8 %copy.7 = f32[896,448]{0,1:T(8,128)} copy(f32[896,448]{1,0:T(8,128)} %get-tuple-element.2) | data formatting | bytes 3211264 | tf_op jit(solution)/shard_map/pallas_call | solution.py:277
  165.9 0.0 copy-done
  165.9 1.7 %copy.9 = f32[2,56,7168]{2,1,0:T(8,128)} copy(f32[2,56,7168]{2,1,0:T(8,128)S(1)} %copy-done) | data formatting | bytes 6422528
Async XLA Ops:
  0.6 2.5 %copy-start.1 = (f32[896,448]{0,1:T(8,128)S(1)}, f32[896,448]{0,1:T(8,128)}, u32[]{:S(2)}) copy-start(f32[896,448]{0,1:T(8,128)} %param.4) | copy-start | bytes 4816900
  163.1 2.8 %copy-start = (f32[2,56,7168]{2,1,0:T(8,128)S(1)}, f32[2,56,7168]{2,1,0:T(8,128)}, u32[]{:S(2)}) copy-start(f32[2,56,7168]{2,1,0:T(8,128)} %get-tuple-element.7) | copy-start | bytes 9633796

commit v2 on v1

v2 whole, which is shorter than its diff:
```python
import functools

import jax
import jax.numpy as jnp
from jax import lax
from jax.experimental import pallas as pl
from jax.experimental.pallas import tpu as pltpu
from jax.sharding import PartitionSpec as P

MESH = pl.DeviceIdType.MESH
EMA_DECAY = 0.9
Q = 7
LEVELS = 32767.0


def encode(values, axis):
    most = jnp.maximum(jnp.max(jnp.abs(values), axis=axis, keepdims=True), 2.0 ** -100)
    power = jnp.ceil(8.0 * jnp.log2(most))
    return jnp.round(jnp.clip(values * jnp.exp2(15.0 - 0.125 * power), -LEVELS, LEVELS)), power


def step_of(power):
    return jnp.exp2(0.125 * power - 15.0)


def pack(values):
    whole, power = encode(values, 0)
    return jnp.concatenate([whole, jnp.broadcast_to(power, (16, power.shape[1]))], axis=0).astype(jnp.int32).astype(jnp.int16)


def unpack(code):
    high = code.shape[0] - 16
    code = code.astype(jnp.int32).astype(jnp.float32)
    return code[:high] * step_of(code[high:high + 1])


def kernel(grad, stats, owner, refreshed, owned, cols, rows, prod, zin, zout, coded, out16, in16,
           g_s, c_s, c_r, b_s, b_r, y_s, y_r, f_s, f_r, k_s, k_r, z_s, z_r, o_s, o_r):
    width, depth = grad.shape
    high = width // Q
    part_w = width // 2
    unit = owned.shape[1]
    dp, tile = lax.axis_index("dp"), lax.axis_index("tile")
    a, z = dp // 4, dp % 4
    b, y, core = tile // 8, (tile // 2) % 4, tile % 2
    middle = a != b

    def at(a_, z_, b_, y_, core_):
        return {"dp": a_ * 4 + z_, "tile": b_ * 8 + y_ * 2 + core_}

    partner = at(1 - a, z, b, y, core)
    bridge = at(1 - a, z, 1 - b, y, core)
    sibling = at(a, z, b, y, 1 - core)
    yu, yd, yo = (y + 1) % 4, (y + 3) % 4, (y + 2) % 4
    zu, zd, zo = (z + 1) % 4, (z + 3) % 4, (z + 2) % 4
    up_y, down_y = at(a, z, b, yu, core), at(a, z, b, yd, core)
    up_z, down_z = at(a, zu, b, y, core), at(a, zd, b, y, core)

    def copy(src, dst, send, recv, device):
        return pltpu.make_async_remote_copy(
            src_ref=src, dst_ref=dst, send_sem=send, recv_sem=recv, device_id=device, device_id_type=MESH
        )

    def c_copy(q):
        place = pl.ds(q * high, high)
        return copy(grad.at[place], cols.at[a, place], c_s.at[q], c_r.at[q], partner)

    def c_arrived(q):
        part = cols.at[1 - a, pl.ds(q * high, high)]
        return copy(part, part, c_s.at[q], c_r.at[q], partner)

    def b_copy(q, which):
        place = pl.ds(q * high, high)
        p = 1 - a if which else a
        return copy(cols.at[p, place] if which else grad.at[place], rows.at[q, core, y, p], b_s.at[q, which], b_r.at[q, which], bridge)

    def b_arrived(q, which):
        part = rows.at[q, core, y, a if which else 1 - a]
        return copy(part, part, b_s.at[q, which], b_r.at[q, which], bridge)

    def y_copy(q, which, p):
        part = rows.at[q, core, y, p]
        return copy(part, part, y_s.at[q, which, p], y_r.at[q, which, p], up_y if which else down_y)

    def y_arrived(q, which, p):
        part = rows.at[q, core, yd if which else yu, p]
        return copy(part, part, y_s.at[q, which, p], y_r.at[q, which, p], up_y if which else down_y)

    def f_copy(q, which):
        part = rows.at[q, core, yd if which else yu, which]
        return copy(part, part, f_s.at[q, which], f_r.at[q, which], up_y if which else down_y)

    def f_arrived(q, which):
        part = rows.at[q, core, yo, which]
        return copy(part, part, f_s.at[q, which], f_r.at[q, which], up_y if which else down_y)

    def k_copy(q, dest, half):
        part = rows.at[q, half, dest]
        return copy(part, part, k_s.at[q, dest], k_r.at[q, dest], sibling)

    def z_copy(q, slot):
        return copy(zout.at[q, slot], zin.at[q, slot], z_s.at[q, slot], z_r.at[q, slot], down_z if slot in (2, 3, 5) else up_z)

    def o_copy(e):
        return copy(out16.at[e], in16.at[tile], o_s.at[e], o_r.at[tile], {"tile": e})

    def o_arrived(e):
        return copy(out16.at[e], in16.at[e], o_s.at[e], o_r.at[e], {"tile": e})

    barrier = pltpu.get_barrier_semaphore()

    def greet(e, _):
        @pl.when(e != tile)
        def _():
            pl.semaphore_signal(barrier, inc=1, device_id={"tile": e}, device_id_type=MESH)
        return 0

    for device in (partner, bridge, up_z, down_z):
        pl.semaphore_signal(barrier, inc=1, device_id=device, device_id_type=MESH)
    lax.fori_loop(0, 16, greet, 0)

    own = pltpu.make_async_copy(grad, cols.at[a], g_s)
    own.start()
    pl.semaphore_wait(barrier, 19)

    def begin(q, _):
        c_copy(q).start()
        return 0

    lax.fori_loop(0, Q, begin, 0)

    @pl.when(middle)
    def _():
        b_copy(0, 0).start()
    own.wait()

    def c_step(q):
        @pl.when(middle & (q > 0))
        def _():
            b_copy(q, 0).start()
        c_arrived(q).wait_recv()

        @pl.when(middle)
        def _():
            b_copy(q, 1).start()

    def ready(q, p, which):
        @pl.when(middle)
        def _():
            b_arrived(q, which).wait_recv()

        @pl.when(jnp.logical_not(middle))
        def _():
            rows[q, core, y, p] = cols[p, pl.ds(pl.multiple_of(q * high, high), high), :]

    def e1(q, which):
        p = jnp.where(middle, 1 - a, a)
        p = 1 - p if which else p
        ready(q, p, which)
        for way in range(2):
            y_copy(q, way, p).start()
        if which:
            k_copy(q, y, core).start()

    def e2(q):
        for which in range(2):
            y_arrived(q, which, which).wait_recv()
            f_copy(q, which).start()
        for which in range(2):
            y_arrived(q, which, 1 - which).wait_recv()
        for dest in (yu, yd):
            k_copy(q, dest, core).start()

    def e3(q):
        for which in range(2):
            f_arrived(q, which).wait_recv()
        k_copy(q, yo, core).start()

    def e4(q):
        for dest in range(4):
            k_copy(q, dest, 1 - core).wait_recv()
        for first in (0, 2):
            total = None
            for p in range(2):
                right = jnp.concatenate([rows[q, half, dest, p] for dest in (first, first + 1) for half in range(2)], axis=0)
                part = lax.dot_general(cols[p], right, (((1,), (1,)), ((), ())), preferred_element_type=jnp.float32)
                total = part if total is None else total + part
            prod[q, first] = total[:, :2 * high]
            prod[q, first + 1] = total[:, 2 * high:]
        for slot, half, dest in ((4, 1, zo), (5, 0, zo), (0, 0, zu), (3, 1, zd)):
            zout[q, slot] = pack(prod[q, dest, half * part_w:(half + 1) * part_w, :])
            z_copy(q, slot).start()

    def e5(q):
        for slot, half, dest in ((1, 1, zu), (2, 0, zd)):
            z_copy(q, 3 + slot).wait_recv()
            zout[q, slot] = pack(prod[q, dest, half * part_w:(half + 1) * part_w, :] + unpack(zin[q, 3 + slot]))
            z_copy(q, slot).start()

    def e6(q):
        for slot in range(4):
            z_copy(q, slot).wait_recv()
        summed = prod[q, z] + jnp.concatenate([unpack(zin[q, k]) + unpack(zin[q, k + 2]) for k in range(2)], axis=0)
        lane = lax.broadcasted_iota(jnp.int32, (width, 2 * high), 1) // high
        places, shifts = [], []
        for half in range(2):
            at_ = half * Q + q
            places.append(pl.ds(pl.multiple_of(at_ // 2 * (2 * high), 2 * high), 2 * high))
            shifts.append((at_ + half) % 2 * high)
        old = [pltpu.roll(stats[:, places[half]], shifts[half], axis=1) for half in range(2)]
        fresh = EMA_DECAY * jnp.where(lane == 0, old[0], old[1]) + (1.0 - EMA_DECAY) * summed
        for half in range(2):
            moved = pltpu.roll(fresh, shifts[half], axis=1)
            refreshed[:, places[half]] = jnp.where(lane == (half * Q + q) % 2, moved, refreshed[:, places[half]])
        across = fresh.T
        pieces, powers = [], []
        for first in range(0, width, 128):
            part = across[:, first:min(first + 128, width)]
            whole, power = encode(part, 1)
            pieces.append(whole)
            powers.append(jnp.broadcast_to(power, (2 * high, 16)))
        code = jnp.concatenate(pieces + powers, axis=1).reshape(2, high // 8, 8, 512)
        for half in range(2):
            coded[pl.ds(half * (width // 8) + q * (high // 8), high // 8)] = code[half]

    def step(i, _):
        def at_step(first, fun):
            pl.when((i >= first) & (i < first + Q))(functools.partial(fun, i - first))

        at_step(0, functools.partial(e1, which=0))
        for k in range(2):
            pl.when(2 * i + k < Q)(functools.partial(c_step, 2 * i + k))
        at_step(0, functools.partial(e1, which=1))
        at_step(1, e2)
        pl.when(i == 4)(functools.partial(e5, 0))
        pl.when((i >= 4) & (i < Q + 3))(functools.partial(e5, i - 3))
        at_step(2, e3)

        pl.when(i == 3)(functools.partial(e4, 0))
        pl.when((i >= 3) & (i < Q + 2))(functools.partial(e4, i - 2))
        pl.when(i == 5)(functools.partial(e6, 0))
        pl.when((i >= 5) & (i < Q + 4))(functools.partial(e6, i - 4))
        return 0

    lax.fori_loop(0, Q + 4, step, 0)

    def peer(j):
        return (b + 1 - j // 8) % 2 * 8 + (y + 1 + j // 2) % 4 * 2 + (core + 1 - j % 2) % 2

    def send(j, _):
        e = peer(j)
        count, first, second = jnp.int32(0), jnp.int32(0), jnp.int32(0)
        for u in range(16):
            mine = (owner[0, u] == e).astype(jnp.int32)
            first = first + jnp.where(count == 0, mine * u, 0)
            second = second + jnp.where(count == 1, mine * u, 0)
            count = count + mine
        pieces = []
        for s, u in enumerate((first, second)):
            held = (count > s).astype(jnp.float32)
            pieces += [coded[u * (unit // 8) + k] * held for k in range(unit // 8)]
        out16[e] = jnp.concatenate(pieces, axis=0).astype(jnp.int32).astype(jnp.int16)

        @pl.when(j < 15)
        def _():
            o_copy(e).start()
        return 0

    lax.fori_loop(0, 16, send, 0)

    def decode(k, _):
        parts = []
        pair = peer(2 * k) // 2
        for c in range(2):
            e = 2 * pair + c

            @pl.when(e != tile)
            def _(e=e):
                o_arrived(e).wait_recv()

            @pl.when(e == tile)
            def _(e=e):
                in16[e] = out16[e]
            got = in16[e].astype(jnp.int32).astype(jnp.float32)
            pieces = []
            for first in range(0, width, 128):
                place = width + 16 * (first // 128)
                scale = jnp.exp2(got[:, place:place + 1] * 0.125) * (1.0 / LEVELS)
                pieces.append(got[:, first:min(first + 128, width)] * scale)
            parts.append(jnp.concatenate(pieces, axis=1))
        both = jnp.concatenate(parts, axis=1)
        for s in range(2):
            owned[s, :, pl.ds(pl.multiple_of(pair * 2 * width, 128), 2 * width)] = both[s * unit:(s + 1) * unit]
        return 0

    lax.fori_loop(0, 8, decode, 0)

    def drain(q, _):
        c_copy(q).wait_send()

        @pl.when(middle)
        def _():
            for which in range(2):
                b_copy(q, which).wait_send()
        for which in range(2):
            for p in range(2):
                y_copy(q, which, p).wait_send()
            f_copy(q, which).wait_send()
        for dest in range(4):
            k_copy(q, dest, core).wait_send()
        for slot in range(6):
            z_copy(q, slot).wait_send()
        return 0

    lax.fori_loop(0, Q, drain, 0)

    def drain_owned(j, _):
        o_copy(peer(j)).wait_send()
        return 0

    lax.fori_loop(0, 15, drain_owned, 0)


def local(gradient, stats_old, owner_map):
    depth, width = gradient.shape
    high = width // Q
    rows = stats_old.shape[0]
    unit = rows // 16
    dma = pltpu.SemaphoreType.DMA
    vmem = pl.BlockSpec(memory_space=pltpu.VMEM)
    refreshed, owned = pl.pallas_call(
        kernel,
        out_shape=(
            jax.ShapeDtypeStruct((width, rows), jnp.float32),
            jax.ShapeDtypeStruct((2, unit, 16 * width), jnp.float32),
        ),
        in_specs=[pl.BlockSpec(memory_space=pl.ANY), vmem, pl.BlockSpec(memory_space=pltpu.SMEM)],
        out_specs=(vmem, vmem),
        scratch_shapes=[
            pltpu.VMEM((2, width, depth), jnp.bfloat16),
            pltpu.VMEM((Q, 2, 4, 2, high, depth), jnp.bfloat16),
            pltpu.VMEM((Q, 4, width, 2 * high), jnp.float32),
            pltpu.VMEM((Q, 6, width // 2 + 16, 2 * high), jnp.int16),
            pltpu.VMEM((Q, 6, width // 2 + 16, 2 * high), jnp.int16),
            pltpu.VMEM((rows // 8, 8, 512), jnp.float32),
            pltpu.VMEM((16, 2 * unit, 512), jnp.int16),
            pltpu.VMEM((16, 2 * unit, 512), jnp.int16),
            dma,
            dma((Q,)), dma((Q,)),
            dma((Q, 2)), dma((Q, 2)),
            dma((Q, 2, 2)), dma((Q, 2, 2)),
            dma((Q, 2)), dma((Q, 2)),
            dma((Q, 4)), dma((Q, 4)),
            dma((Q, 6)), dma((Q, 6)),
            dma((16,)), dma((16,)),
        ],
        compiler_params=pltpu.CompilerParams(
            collective_id=0, has_side_effects=True, vmem_limit_bytes=60 << 20
        ),
    )(gradient.T, stats_old.T, owner_map)
    return refreshed.T, owned


def solution(mesh):
    return jax.shard_map(
        local,
        mesh=mesh,
        in_specs=(P("dp", "tile"), P("dp", "tile"), P("dp", None)),
        out_specs=(P("dp", "tile"), P(("dp", "tile"), None, None)),
        check_vma=False,
    )
```

time: 170 us -> 132 us (0.78); the launches traced: 168 us -> 132 us
  Pallas kernels: 158 us -> 127 us
  local copies, waits for them, and re-layouts: 8.7 us -> 4.52 us
    pallas_call x1, Pallas kernels: 158 us -> 127 us  [local(): pl.pallas_call(kernel, out_shape=(jax.ShapeDtypeStruct((width, rows), jnp...]
    pallas_call x1 -> x0, local copies, waits for them, and re-layouts: 2.8 us -> none  [local(): pl.pallas_call(kernel, out_shape=(jax.ShapeDtypeStruct((rows, width), jnp...]
    unnamed x7 -> x4, local copies, waits for them, and re-layouts: 5.9 us -> 4.52 us
where the time goes in v2:
time: 132 us
  Pallas kernels  127 us (96%)
  local copies, waits for them, and re-layouts  4.52 us (3%)
    pallas_call x1, Pallas kernels, local(): pl.pallas_call(kernel, out_shape=(jax.ShapeDtypeStruct((width, rows), jnp...  127 us
    unnamed x4, local copies, waits for them, and re-layouts  4.52 us

profile of v2, /device:TPU:24, one launch (start us, length us, event | category | flops | bytes accessed | tf_op | source)
XLA Modules:
  0.0 132.1 jit_solution(2107495286695511381)
XLA Ops:
  0.6 126.9 %shard_map.50 = (f32[448,896]{1,0:T(8,128)}, f32[2,56,7168]{2,1,0:T(8,128)}) custom-call(bf16[448,1152]{1,0:T(8,128)(2,1)} %bitcast.5, f32[448,896]{1,0:T(8,128)} %bitcast.3, s32[1,16]{1,0:T(1,128)} %owner.1), custom_call_target="tpu_custom_call" | custom-call | tf_op jit(solution)/shard_map/pallas_call | solution.py:331
  127.5 0.0 copy-start
  127.6 2.8 %copy.7 = f32[896,448]{0,1:T(8,128)} copy(f32[896,448]{0,1:T(8,128)} %bitcast.4) | data formatting | bytes 3211264
  130.4 0.0 copy-done
  130.4 1.7 %copy.8 = f32[2,56,7168]{2,1,0:T(8,128)} copy(f32[2,56,7168]{2,1,0:T(8,128)S(1)} %copy-done) | data formatting | bytes 6422528
Async XLA Ops:
  127.5 2.8 %copy-start = (f32[2,56,7168]{2,1,0:T(8,128)S(1)}, f32[2,56,7168]{2,1,0:T(8,128)}, u32[]{:S(2)}) copy-start(f32[2,56,7168]{2,1,0:T(8,128)} %get-tuple-element.9) | copy-start | bytes 9633796

commit v3 on v2

--- a/solution.py
+++ b/solution.py
@@ -10,6 +10,7 @@
 MESH = pl.DeviceIdType.MESH
 EMA_DECAY = 0.9
 Q = 7
+STEPS = 2
 LEVELS = 32767.0
 
 
@@ -34,12 +35,12 @@
     return code[:high] * step_of(code[high:high + 1])
 
 
-def kernel(grad, stats, owner, refreshed, owned, cols, rows, prod, zin, zout, coded, out16, in16,
-           g_s, c_s, c_r, b_s, b_r, y_s, y_r, f_s, f_r, k_s, k_r, z_s, z_r, o_s, o_r):
+def kernel(grad, stats_in, owner, refreshed_out, in16, cols, rows, stats, refreshed, prod, zin, zout, coded, out16,
+           g_s, t_s, w_s, m_s, c_s, c_r, b_s, b_r, y_s, y_r, f_s, f_r, k_s, k_r, z_s, z_r, o_s, o_r):
     width, depth = grad.shape
     high = width // Q
     part_w = width // 2
-    unit = owned.shape[1]
+    unit = in16.shape[1] // 2
     dp, tile = lax.axis_index("dp"), lax.axis_index("tile")
     a, z = dp // 4, dp % 4
     b, y, core = tile // 8, (tile // 2) % 4, tile % 2
@@ -121,17 +122,18 @@
 
     own = pltpu.make_async_copy(grad, cols.at[a], g_s)
     own.start()
+    old_stats = pltpu.make_async_copy(stats_in, stats, t_s)
+    old_stats.start()
     pl.semaphore_wait(barrier, 19)
 
     def begin(q, _):
         c_copy(q).start()
         return 0
-
-    lax.fori_loop(0, Q, begin, 0)
 
     @pl.when(middle)
     def _():
         b_copy(0, 0).start()
+    lax.fori_loop(0, Q, begin, 0)
     own.wait()
 
     def c_step(q):
@@ -232,17 +234,20 @@
             pl.when(2 * i + k < Q)(functools.partial(c_step, 2 * i + k))
         at_step(0, functools.partial(e1, which=1))
         at_step(1, e2)
+        at_step(2, e3)
+        pl.when(i == 3)(functools.partial(e4, 0))
+        pl.when((i >= 3) & (i < Q + 2))(functools.partial(e4, i - 2))
         pl.when(i == 4)(functools.partial(e5, 0))
         pl.when((i >= 4) & (i < Q + 3))(functools.partial(e5, i - 3))
-        at_step(2, e3)
-
-        pl.when(i == 3)(functools.partial(e4, 0))
-        pl.when((i >= 3) & (i < Q + 2))(functools.partial(e4, i - 2))
+        pl.when(i == 4)(old_stats.wait)
         pl.when(i == 5)(functools.partial(e6, 0))
         pl.when((i >= 5) & (i < Q + 4))(functools.partial(e6, i - 4))
         return 0
 
     lax.fori_loop(0, Q + 4, step, 0)
+
+    done = pltpu.make_async_copy(refreshed, refreshed_out, w_s)
+    done.start()
 
     def peer(j):
         return (b + 1 - j // 8) % 2 * 8 + (y + 1 + j // 2) % 4 * 2 + (core + 1 - j % 2) % 2
@@ -268,32 +273,16 @@
 
     lax.fori_loop(0, 16, send, 0)
 
-    def decode(k, _):
-        parts = []
-        pair = peer(2 * k) // 2
-        for c in range(2):
-            e = 2 * pair + c
-
-            @pl.when(e != tile)
-            def _(e=e):
-                o_arrived(e).wait_recv()
-
-            @pl.when(e == tile)
-            def _(e=e):
-                in16[e] = out16[e]
-            got = in16[e].astype(jnp.int32).astype(jnp.float32)
-            pieces = []
-            for first in range(0, width, 128):
-                place = width + 16 * (first // 128)
-                scale = jnp.exp2(got[:, place:place + 1] * 0.125) * (1.0 / LEVELS)
-                pieces.append(got[:, first:min(first + 128, width)] * scale)
-            parts.append(jnp.concatenate(pieces, axis=1))
-        both = jnp.concatenate(parts, axis=1)
-        for s in range(2):
-            owned[s, :, pl.ds(pl.multiple_of(pair * 2 * width, 128), 2 * width)] = both[s * unit:(s + 1) * unit]
-        return 0
-
-    lax.fori_loop(0, 8, decode, 0)
+    kept = pltpu.make_async_copy(out16.at[tile], in16.at[tile], m_s)
+    kept.start()
+
+    def arrive(j, _):
+        o_arrived(peer(j)).wait_recv()
+        return 0
+
+    lax.fori_loop(0, 15, arrive, 0)
+    kept.wait()
+    done.wait()
 
     def drain(q, _):
         c_copy(q).wait_send()
@@ -321,31 +310,50 @@
     lax.fori_loop(0, 15, drain_owned, 0)
 
 
+def finish(refreshed, in16, refreshed_out, owned):
+    refreshed_out[...] = refreshed[...]
+    unit = owned.shape[1]
+    tiles = 16 // STEPS
+    width = owned.shape[2] // tiles
+    parts = []
+    for c in range(tiles):
+        got = in16[c].astype(jnp.int32).astype(jnp.float32)
+        pieces = []
+        for first in range(0, width, 128):
+            place = width + 16 * (first // 128)
+            pieces.append(got[:, first:min(first + 128, width)] * step_of(got[:, place:place + 1]))
+        parts.append(jnp.concatenate(pieces, axis=1))
+    both = jnp.concatenate(parts, axis=1)
+    for s in range(2):
+        owned[s] = both[s * unit:(s + 1) * unit]
+
+
 def local(gradient, stats_old, owner_map):
     depth, width = gradient.shape
     high = width // Q
     rows = stats_old.shape[0]
     unit = rows // 16
     dma = pltpu.SemaphoreType.DMA
-    vmem = pl.BlockSpec(memory_space=pltpu.VMEM)
-    refreshed, owned = pl.pallas_call(
+    hbm = pl.BlockSpec(memory_space=pl.ANY)
+    refreshed, in16 = pl.pallas_call(
         kernel,
         out_shape=(
             jax.ShapeDtypeStruct((width, rows), jnp.float32),
-            jax.ShapeDtypeStruct((2, unit, 16 * width), jnp.float32),
+            jax.ShapeDtypeStruct((16, 2 * unit, 512), jnp.int16),
         ),
-        in_specs=[pl.BlockSpec(memory_space=pl.ANY), vmem, pl.BlockSpec(memory_space=pltpu.SMEM)],
-        out_specs=(vmem, vmem),
+        in_specs=[hbm, hbm, pl.BlockSpec(memory_space=pltpu.SMEM)],
+        out_specs=(hbm, hbm),
         scratch_shapes=[
             pltpu.VMEM((2, width, depth), jnp.bfloat16),
             pltpu.VMEM((Q, 2, 4, 2, high, depth), jnp.bfloat16),
+            pltpu.VMEM((width, rows), jnp.float32),
+            pltpu.VMEM((width, rows), jnp.float32),
             pltpu.VMEM((Q, 4, width, 2 * high), jnp.float32),
             pltpu.VMEM((Q, 6, width // 2 + 16, 2 * high), jnp.int16),
             pltpu.VMEM((Q, 6, width // 2 + 16, 2 * high), jnp.int16),
             pltpu.VMEM((rows // 8, 8, 512), jnp.float32),
             pltpu.VMEM((16, 2 * unit, 512), jnp.int16),
-            pltpu.VMEM((16, 2 * unit, 512), jnp.int16),
-            dma,
+            dma, dma, dma, dma,
             dma((Q,)), dma((Q,)),
             dma((Q, 2)), dma((Q, 2)),
             dma((Q, 2, 2)), dma((Q, 2, 2)),
@@ -358,6 +366,23 @@
             collective_id=0, has_side_effects=True, vmem_limit_bytes=60 << 20
         ),
     )(gradient.T, stats_old.T, owner_map)
+    refreshed, owned = pl.pallas_call(
+        finish,
+        grid=(STEPS,),
+        out_shape=(
+            jax.ShapeDtypeStruct((width, rows), jnp.float32),
+            jax.ShapeDtypeStruct((2, unit, 16 * width), jnp.float32),
+        ),
+        in_specs=[
+            pl.BlockSpec((width // STEPS, rows), lambda i: (i, 0)),
+            pl.BlockSpec((16 // STEPS, 2 * unit, 512), lambda i: (i, 0, 0)),
+        ],
+        out_specs=(
+            pl.BlockSpec((width // STEPS, rows), lambda i: (i, 0)),
+            pl.BlockSpec((2, unit, 16 // STEPS * width), lambda i: (0, 0, i)),
+        ),
+        compiler_params=pltpu.CompilerParams(vmem_limit_bytes=60 << 20),
+    )(refreshed, in16)
     return refreshed.T, owned
 
 

time: 132 us -> 127 us (0.962)
  local copies, waits for them, and re-layouts: 4.52 us -> 0 us
    pallas_call x1, Pallas kernels: 127 us -> 121 us  [local(): pl.pallas_call(kernel, out_shape=(jax.ShapeDtypeStruct((width, rows), jnp...]
    unnamed x4 -> x0, local copies, waits for them, and re-layouts: 4.52 us -> none
    pallas_call x0 -> x1, Pallas kernels: none -> 4.52 us  [local(): pl.pallas_call(finish, grid=(STEPS,), out_shape=(jax.ShapeDtypeStruct((wi...]
where the time goes in v3:
time: 127 us; the launch traced here: 126 us
  Pallas kernels  126 us (99%)
    pallas_call x1, Pallas kernels, local(): pl.pallas_call(kernel, out_shape=(jax.ShapeDtypeStruct((width, rows), jnp...  121 us
    pallas_call x1, Pallas kernels, local(): pl.pallas_call(finish, grid=(STEPS,), out_shape=(jax.ShapeDtypeStruct((wi...  4.52 us

profile of v3, /device:TPU:24, one launch (start us, length us, event | category | flops | bytes accessed | tf_op | source)
XLA Modules:
  0.0 126.3 jit_solution(1584325851420815346)
XLA Ops:
  0.6 121.1 %shard_map.50 = (f32[448,896]{1,0:T(8,128)}, s16[16,112,512]{2,1,0:T(8,128)(2,1)}) custom-call(bf16[448,1152]{1,0:T(8,128)(2,1)} %bitcast.4, f32[448,896]{1,0:T(8,128)} %bitcast.3, s32[1,16]{1,0:T(1,128)} %owner.1), custom_call_target="tpu_custom_call" | custom-call | tf_op jit(solution)/shard_map/pallas_call | solution.py:338
  121.8 4.5 %shard_map.51 = (f32[448,896]{1,0:T(8,128)}, f32[2,56,7168]{2,1,0:T(8,128)}) custom-call(f32[448,896]{1,0:T(8,128)} %get-tuple-element.6.refreshed, s16[16,112,512]{2,1,0:T(8,128)(2,1)} %get-tuple-element.7.in16), custom_call_target="tpu_custom_call" | custom-call | tf_op jit(solution)/shard_map/pallas_call | solution.py:369

commit v4 on v3

--- a/solution.py
+++ b/solution.py
@@ -178,20 +178,29 @@
             f_arrived(q, which).wait_recv()
         k_copy(q, yo, core).start()
 
-    def e4(q):
-        for dest in range(4):
-            k_copy(q, dest, 1 - core).wait_recv()
-        for first in (0, 2):
-            total = None
-            for p in range(2):
-                right = jnp.concatenate([rows[q, half, dest, p] for dest in (first, first + 1) for half in range(2)], axis=0)
-                part = lax.dot_general(cols[p], right, (((1,), (1,)), ((), ())), preferred_element_type=jnp.float32)
-                total = part if total is None else total + part
-            prod[q, first] = total[:, :2 * high]
-            prod[q, first + 1] = total[:, 2 * high:]
-        for slot, half, dest in ((4, 1, zo), (5, 0, zo), (0, 0, zu), (3, 1, zd)):
-            zout[q, slot] = pack(prod[q, dest, half * part_w:(half + 1) * part_w, :])
-            z_copy(q, slot).start()
+    def product(q, dest):
+        k_copy(q, dest, 1 - core).wait_recv()
+        total = None
+        for p in range(2):
+            right = jnp.concatenate([rows[q, half, dest, p] for half in range(2)], axis=0)
+            part = lax.dot_general(cols[p], right, (((1,), (1,)), ((), ())), preferred_element_type=jnp.float32)
+            total = part if total is None else total + part
+        prod[q, dest] = total
+        for slot, half, goal in ((4, 1, zo), (5, 0, zo), (0, 0, zu), (3, 1, zd)):
+            @pl.when(dest == goal)
+            def _(slot=slot, half=half):
+                zout[q, slot] = pack(total[half * part_w:(half + 1) * part_w])
+                z_copy(q, slot).start()
+
+    def e4a(q):
+        def one(k, _):
+            product(q, jnp.where(k == 0, y, jnp.where(k == 1, yu, yd)))
+            return 0
+
+        lax.fori_loop(0, 3, one, 0)
+
+    def e4b(q):
+        product(q, yo)
 
     def e5(q):
         for slot, half, dest in ((1, 1, zu), (2, 0, zd)):
@@ -234,9 +243,11 @@
             pl.when(2 * i + k < Q)(functools.partial(c_step, 2 * i + k))
         at_step(0, functools.partial(e1, which=1))
         at_step(1, e2)
+        pl.when(i == 3)(functools.partial(e4a, 0))
+        pl.when(i == 3)(functools.partial(e4b, 0))
+        pl.when((i >= 3) & (i < Q + 2))(functools.partial(e4a, i - 2))
         at_step(2, e3)
-        pl.when(i == 3)(functools.partial(e4, 0))
-        pl.when((i >= 3) & (i < Q + 2))(functools.partial(e4, i - 2))
+        pl.when((i >= 3) & (i < Q + 2))(functools.partial(e4b, i - 2))
         pl.when(i == 4)(functools.partial(e5, 0))
         pl.when((i >= 4) & (i < Q + 3))(functools.partial(e5, i - 3))
         pl.when(i == 4)(old_stats.wait)

time: 127 us -> 126 us (level); the launches traced: 126 us -> 124 us
  Pallas kernels: 126 us -> 123 us
    pallas_call x1, Pallas kernels: 121 us -> 118 us  [local(): pl.pallas_call(kernel, out_shape=(jax.ShapeDtypeStruct((width, rows), jnp...]
where the time goes in v4:
time: 126 us; the launch traced here: 124 us
  Pallas kernels  123 us (98%)
    pallas_call x1, Pallas kernels, local(): pl.pallas_call(kernel, out_shape=(jax.ShapeDtypeStruct((width, rows), jnp...  118 us
    pallas_call x1, Pallas kernels, local(): pl.pallas_call(finish, grid=(STEPS,), out_shape=(jax.ShapeDtypeStruct((wi...  4.52 us

profile of v4, /device:TPU:24, one launch (start us, length us, event | category | flops | bytes accessed | tf_op | source)
XLA Modules:
  0.0 123.7 jit_solution(8017842844786259145)
XLA Ops:
  0.6 118.5 %shard_map.50 = (f32[448,896]{1,0:T(8,128)}, s16[16,112,512]{2,1,0:T(8,128)(2,1)}) custom-call(bf16[448,1152]{1,0:T(8,128)(2,1)} %bitcast.4, f32[448,896]{1,0:T(8,128)} %bitcast.3, s32[1,16]{1,0:T(1,128)} %owner.1), custom_call_target="tpu_custom_call" | custom-call | tf_op jit(solution)/shard_map/pallas_call | solution.py:349
  119.1 4.5 %shard_map.51 = (f32[448,896]{1,0:T(8,128)}, f32[2,56,7168]{2,1,0:T(8,128)}) custom-call(f32[448,896]{1,0:T(8,128)} %get-tuple-element.6.refreshed, s16[16,112,512]{2,1,0:T(8,128)(2,1)} %get-tuple-element.7.in16), custom_call_target="tpu_custom_call" | custom-call | tf_op jit(solution)/shard_map/pallas_call | solution.py:380

commit v5 on v4

--- a/solution.py
+++ b/solution.py
@@ -40,7 +40,7 @@
     width, depth = grad.shape
     high = width // Q
     part_w = width // 2
-    unit = in16.shape[1] // 2
+    unit = 8 * coded.shape[0] // 16
     dp, tile = lax.axis_index("dp"), lax.axis_index("tile")
     a, z = dp // 4, dp % 4
     b, y, core = tile // 8, (tile // 2) % 4, tile % 2
@@ -263,6 +263,8 @@
     def peer(j):
         return (b + 1 - j // 8) % 2 * 8 + (y + 1 + j // 2) % 4 * 2 + (core + 1 - j % 2) % 2
 
+    whole = width // 128 * 128
+
     def send(j, _):
         e = peer(j)
         count, first, second = jnp.int32(0), jnp.int32(0), jnp.int32(0)
@@ -275,7 +277,12 @@
         for s, u in enumerate((first, second)):
             held = (count > s).astype(jnp.float32)
             pieces += [coded[u * (unit // 8) + k] * held for k in range(unit // 8)]
-        out16[e] = jnp.concatenate(pieces, axis=0).astype(jnp.int32).astype(jnp.int16)
+        both = jnp.concatenate(pieces, axis=0)
+        tail = jnp.concatenate([both[:unit, whole:width], both[unit:, whole:width]], axis=1)
+        scales = jnp.concatenate([both[:, width:], jnp.zeros((128 - 2 * unit, 512 - width), jnp.float32)], axis=0).T
+        scales = jnp.concatenate([scales[16 * k:16 * k + 1] for k in range(4)] + [jnp.zeros((4, 128), jnp.float32)], axis=0)
+        tiles = [both[:, first:first + 128] for first in range(0, whole, 128)]
+        out16[e] = jnp.concatenate(tiles + [tail, scales], axis=0).astype(jnp.int32).astype(jnp.int16)
 
         @pl.when(j < 15)
         def _():
@@ -327,12 +334,16 @@
     tiles = 16 // STEPS
     width = owned.shape[2] // tiles
     parts = []
+    count = width // 128
     for c in range(tiles):
         got = in16[c].astype(jnp.int32).astype(jnp.float32)
-        pieces = []
-        for first in range(0, width, 128):
-            place = width + 16 * (first // 128)
-            pieces.append(got[:, first:min(first + 128, width)] * step_of(got[:, place:place + 1]))
+        tail = got[2 * unit * count:2 * unit * count + unit]
+        scales = got[2 * unit * count + unit:]
+        scales = step_of(jnp.concatenate([scales, jnp.zeros((128 - scales.shape[0], 128), jnp.float32)], axis=0).T)
+        pieces = [got[2 * unit * k:2 * unit * (k + 1)] * scales[:2 * unit, k:k + 1] for k in range(count)]
+        rest = width - 128 * count
+        last = jnp.concatenate([tail[:, :rest], tail[:, rest:2 * rest]], axis=0)
+        pieces.append(last * scales[:2 * unit, count:count + 1])
         parts.append(jnp.concatenate(pieces, axis=1))
     both = jnp.concatenate(parts, axis=1)
     for s in range(2):
@@ -350,7 +361,7 @@
         kernel,
         out_shape=(
             jax.ShapeDtypeStruct((width, rows), jnp.float32),
-            jax.ShapeDtypeStruct((16, 2 * unit, 512), jnp.int16),
+            jax.ShapeDtypeStruct((16, 2 * unit * (width // 128) + unit + 8, 128), jnp.int16),
         ),
         in_specs=[hbm, hbm, pl.BlockSpec(memory_space=pltpu.SMEM)],
         out_specs=(hbm, hbm),
@@ -363,7 +374,7 @@
             pltpu.VMEM((Q, 6, width // 2 + 16, 2 * high), jnp.int16),
             pltpu.VMEM((Q, 6, width // 2 + 16, 2 * high), jnp.int16),
             pltpu.VMEM((rows // 8, 8, 512), jnp.float32),
-            pltpu.VMEM((16, 2 * unit, 512), jnp.int16),
+            pltpu.VMEM((16, 2 * unit * (width // 128) + unit + 8, 128), jnp.int16),
             dma, dma, dma, dma,
             dma((Q,)), dma((Q,)),
             dma((Q, 2)), dma((Q, 2)),
@@ -386,7 +397,7 @@
         ),
         in_specs=[
             pl.BlockSpec((width // STEPS, rows), lambda i: (i, 0)),
-            pl.BlockSpec((16 // STEPS, 2 * unit, 512), lambda i: (i, 0, 0)),
+            pl.BlockSpec((16 // STEPS, 2 * unit * (width // 128) + unit + 8, 128), lambda i: (i, 0, 0)),
         ],
         out_specs=(
             pl.BlockSpec((width // STEPS, rows), lambda i: (i, 0)),

time: 126 us -> 124 us (0.984)
    pallas_call x1, Pallas kernels: 118 us -> 117 us  [local(): pl.pallas_call(kernel, out_shape=(jax.ShapeDtypeStruct((width, rows), jnp...]
where the time goes in v5:
time: 124 us; the launch traced here: 122 us
  Pallas kernels  122 us (98%)
    pallas_call x1, Pallas kernels, local(): pl.pallas_call(kernel, out_shape=(jax.ShapeDtypeStruct((width, rows), jnp...  117 us
    pallas_call x1, Pallas kernels, local(): pl.pallas_call(finish, grid=(STEPS,), out_shape=(jax.ShapeDtypeStruct((wi...  5.01 us

profile of v5, /device:TPU:24, one launch (start us, length us, event | category | flops | bytes accessed | tf_op | source)
XLA Modules:
  0.0 122.2 jit_solution(12143530166984864994)
XLA Ops:
  0.6 116.5 %shard_map.50 = (f32[448,896]{1,0:T(8,128)}, s16[16,400,128]{2,1,0:T(8,128)(2,1)}) custom-call(bf16[448,1152]{1,0:T(8,128)(2,1)} %bitcast.4, f32[448,896]{1,0:T(8,128)} %bitcast.3, s32[1,16]{1,0:T(1,128)} %owner.1), custom_call_target="tpu_custom_call" | custom-call | tf_op jit(solution)/shard_map/pallas_call | solution.py:360
  117.2 5.0 %shard_map.51 = (f32[448,896]{1,0:T(8,128)}, f32[2,56,7168]{2,1,0:T(8,128)}) custom-call(f32[448,896]{1,0:T(8,128)} %get-tuple-element.6.refreshed, s16[16,400,128]{2,1,0:T(8,128)(2,1)} %get-tuple-element.7.in16), custom_call_target="tpu_custom_call" | custom-call | tf_op jit(solution)/shard_map/pallas_call | solution.py:391

commit v6 on v5

--- a/solution.py
+++ b/solution.py
@@ -10,7 +10,7 @@
 MESH = pl.DeviceIdType.MESH
 EMA_DECAY = 0.9
 Q = 7
-STEPS = 2
+STEPS = 4
 LEVELS = 32767.0
 
 

time: 124 us -> 125 us (level)
  no operation moved by 1% of the time
where the time goes in v6:
time: 125 us; the launch traced here: 123 us
  Pallas kernels  122 us (98%)
    pallas_call x1, Pallas kernels, local(): pl.pallas_call(kernel, out_shape=(jax.ShapeDtypeStruct((width, rows), jnp...  117 us
    pallas_call x1, Pallas kernels, local(): pl.pallas_call(finish, grid=(STEPS,), out_shape=(jax.ShapeDtypeStruct((wi...  5.65 us

profile of v6, /device:TPU:24, one launch (start us, length us, event | category | flops | bytes accessed | tf_op | source)
XLA Modules:
  0.0 122.8 jit_solution(2313428530318427595)
XLA Ops:
  0.6 116.5 %shard_map.50 = (f32[448,896]{1,0:T(8,128)}, s16[16,400,128]{2,1,0:T(8,128)(2,1)}) custom-call(bf16[448,1152]{1,0:T(8,128)(2,1)} %bitcast.4, f32[448,896]{1,0:T(8,128)} %bitcast.3, s32[1,16]{1,0:T(1,128)} %owner.1), custom_call_target="tpu_custom_call" | custom-call | tf_op jit(solution)/shard_map/pallas_call | solution.py:360
  117.2 5.7 %shard_map.51 = (f32[448,896]{1,0:T(8,128)}, f32[2,56,7168]{2,1,0:T(8,128)}) custom-call(f32[448,896]{1,0:T(8,128)} %get-tuple-element.6.refreshed, s16[16,400,128]{2,1,0:T(8,128)(2,1)} %get-tuple-element.7.in16), custom_call_target="tpu_custom_call" | custom-call | tf_op jit(solution)/shard_map/pallas_call | solution.py:391
